TPU v7x, 256 devices: a whole 4x4x8 slice. The times are simulated.
256 devices in a mesh: pb: 8 (over z), col: 32 (over y, x, core).
Axes of the slice: x: 4, y: 4, z: 8, core: 2. Of those that a mesh axis runs over, the one named last changes fastest.
Arguments:
- queries: bfloat16 [16384, 512], P('pb'), may hold values from -0.29882812 to 0.29882812
- positive: int32 [16384], P('pb'), may hold values from 0 to 16383, each once
- items: bfloat16 [16384, 512], P('col'), may hold values from -0.29882812 to 0.29882812
- item_counts: int32 [16384], P('col'), may hold values from 1 to 189
- cache: bfloat16 [32768, 512], P('col'), may hold values from -0.29882812 to 0.29882812
- neg_owner: int32 [16384, 1], P('col'), may hold values from 0 to 31; in each aligned block of 512 rows (0 to 511, 512 to 1023, ...) at most 32 rows name the same one
- neg_row: int32 [16384], P('col'), may hold values from 0 to 1023
- neg_counts: int32 [16384], P('col'), may hold values from 1 to 189
Outputs:
- query_loss: float32 [16384], P('pb')
- query_grad: float32 [16384, 512], P(('pb', 'col'))
- item_grad: float32 [16384, 512], P('col')
- cache_grad: float32 [32768, 512], P('col')
Inputs may be any that keep to these rules, and one draw needn't show every extreme that they name: `neg_owner`: within the 512 rows of one index of col no owner is named more than 32 times.
All inputs are finite; a program needn't handle non-finite values.
Results may differ from a plain program's by a relative error of at most 0.0009.
The roundings to bfloat16 on the way count: a program that leaves them out, or rounds other values in their place, can miss the bound.
Values may be sent and summed in bfloat16 or wider, within the bound.
A program may use at most 64 MiB of HBM per device.

v0:
```python
import jax
import jax.numpy as jnp
from jax import lax
from jax.experimental import pallas as pl
from jax.experimental.pallas import tpu as pltpu
from jax.sharding import PartitionSpec as P

MESH = pl.DeviceIdType.MESH
F32 = jnp.float32
BF16 = jnp.bfloat16
I32 = jnp.int32
I16 = jnp.int16

E = 512
H = E // 2
NQ = 2048
QB = 256
NB = NQ // QB
NI = 512
NN = 512
NS = 1024
NC = 32
NZ = 8
CAP = 32
ROWS = 1024
CH = 64
INV_T = 20.0
PB = 4
W = E // 4
CR = ROWS // NZ
LN2 = 0.6931471805599453
SCALE2 = INV_T / LN2


def iota(shape, dim):
    return lax.broadcasted_iota(I32, shape, dim)


def onehot(cond):
    return jnp.where(cond, 1.0, 0.0).astype(BF16)


def dot_nn(a, b):
    return lax.dot_general(a, b, (((1,), (0,)), ((), ())), preferred_element_type=F32)


def dot_nt(a, b):
    return lax.dot_general(a, b, (((1,), (1,)), ((), ())), preferred_element_type=F32)


def dot_tn(a, b):
    return lax.dot_general(a, b, (((0,), (0,)), ((), ())), preferred_element_type=F32)


def halves(x):
    hi = x.astype(BF16)
    return hi, (x - hi.astype(F32)).astype(BF16)


def encode(x, group):
    rows, width = x.shape
    cube = x.reshape(rows // group, group, width)
    top = jnp.max(jnp.abs(cube), axis=0)
    expo = jnp.ceil(jnp.log2(jnp.maximum(top, 1e-30)))
    code = jnp.round(cube * jnp.exp2(14.99 - expo)[None])
    return code.reshape(rows, width).astype(I32).astype(I16), expo


def decode(code, expo):
    rows, width = code.shape
    group = expo.shape[0]
    cube = code.astype(I32).astype(F32).reshape(rows // group, group, width)
    return (cube * jnp.exp2(expo - 14.99)[None]).reshape(rows, width)


def to_i16(x):
    return x.astype(I32).astype(I16)


def from_i16(x):
    return x.astype(I32).astype(F32)


def unit(x):
    scale = jnp.sqrt(jnp.sum(x * x, axis=1, keepdims=True) + 1e-06)
    return x * (1.0 / scale), scale


def unit_back(grad, rows):
    direction, scale = unit(rows)
    return (grad - direction * jnp.sum(grad * direction, axis=1, keepdims=True)) / scale


def kernel(
    queries_hbm, positive_hbm, items_hbm, counts_i_hbm, counts_n_hbm, owner_hbm, row_hbm, cache_hbm,
    loss_out, query_out, item_codes, cache_codes,
    queries, positive, items, counts_i_ref, counts_n_ref, owner_ref, row_ref, cache, loss_buf, query_buf, msg, mrecv, cache_unit, scat, q_unit, cand_i, cand_n, shift_n,
    expo_i, expo_n, pos, tot, sums_i, factor_i, factor_n, weight_i, weight_n, part_i, part_n,
    slot_grad, slot_hi, slot_lo,
    send_i, recv_i, send_n, recv_n, ag_item, ag_cache, q_part, q_core, q_msg, q_recv,
    in_s, m_s, m_r, p_s, p_r, t_s, t_r, ri_s, ri_r, rn_s, rn_r, ai_s, ai_r, ac_s, ac_r, oi_s, oc_s,
    qc_s, qc_r, qd_s, qd_r, out_s,
):
    me = lax.axis_index("col")
    z = lax.axis_index("pb")
    core = me % 2
    chip = me // 2
    my_g = me // 4
    up = (z + 1) % NZ
    down = (z + NZ - 1) % NZ
    sibling = chip * 2 + 1 - core

    barrier = pltpu.get_barrier_semaphore()
    loads = [
        pltpu.make_async_copy(src, dst, in_s.at[i])
        for i, (src, dst) in enumerate(
            (
                (owner_hbm, owner_ref),
                (row_hbm, row_ref),
                (counts_n_hbm, counts_n_ref),
                (counts_i_hbm, counts_i_ref),
                (items_hbm, items),
                (positive_hbm, positive),
                (queries_hbm, queries),
                (cache_hbm, cache),
            )
        )
    ]
    for load in loads:
        load.start()

    @pl.loop(1, NC)
    def _(s):
        pl.semaphore_signal(barrier, inc=1, device_id={"col": (me + s) % NC}, device_id_type=MESH)

    for other in (up, down):
        pl.semaphore_signal(barrier, inc=1, device_id={"pb": other}, device_id_type=MESH)

    def remote(src, dst, send, recv, **where):
        return pltpu.make_async_remote_copy(
            src_ref=src, dst_ref=dst, send_sem=send, recv_sem=recv, device_id=where, device_id_type=MESH
        )

    def pair_row(ref, b):
        return jnp.concatenate([ref[pl.ds(2 * b, 1), :], ref[pl.ds(2 * b + 1, 1), :]], axis=1)

    def put_pair(ref, b, value):
        ref[pl.ds(2 * b, 1), :] = value[:, 0:128]
        ref[pl.ds(2 * b + 1, 1), :] = value[:, 128:]

    for load in loads[0:4]:
        load.wait()
    counts_i = counts_i_ref[...].astype(F32)
    counts_n = counts_n_ref[...].astype(F32)
    owner = owner_ref[...]
    row = row_ref[...]
    table = jnp.where(iota((NC, NN), 0) == owner, 1.0, 0.0)
    before = onehot(iota((NN, NN), 0) < iota((NN, NN), 1))
    earlier = dot_nn(table.astype(BF16), before)
    rank = jnp.sum(earlier * table, axis=0, keepdims=True).astype(I32)
    lane = onehot(iota((128, NN), 0) == CAP * (me % 4) + rank)
    named = jnp.concatenate(
        [table * (row >> 5).astype(F32), table * (row & 31).astype(F32), table * counts_n], axis=0
    )
    named = dot_nt(named.astype(BF16), lane)
    named = named[0:NC] * 32.0 + named[NC : 2 * NC] + named[2 * NC :] * ROWS
    total_i = jnp.sum(counts_i, axis=1, keepdims=True).reshape(1, 1, 1)
    total_n = jnp.sum(counts_n, axis=1, keepdims=True).reshape(1, 1, 1)
    line = iota((NC, 8, 128), 1)
    totals = jnp.where(line == (my_g + 1) % 8, total_i, jnp.where(line == (my_g + 2) % 8, total_n, 0.0))
    msg[...] = jnp.where(line == my_g, named.reshape(NC, 1, 128), totals)

    pl.semaphore_wait(barrier, NC + 1)

    def to_all(ref, send, recv, s):
        other = (me + s) % NC
        return remote(ref.at[me], ref.at[me], send.at[other], recv.at[me], col=other)

    def from_all(ref, send, recv, s):
        other = (me + s) % NC
        return remote(ref.at[me], ref.at[other], send.at[other], recv.at[other], col=other)

    @pl.loop(1, NC)
    def _(s):
        other = (me + s) % NC
        remote(msg.at[other], mrecv.at[me], m_s.at[other], m_r.at[me], col=other).start()

    mrecv[me] = msg[me]

    loads[4].wait()
    cand_i[...] = unit(items[...].astype(F32))[0].astype(BF16)
    same = iota((NI, NI), 0) == iota((NI, NI), 1)
    shift_i = jnp.log2(jnp.sum(jnp.where(same, counts_i, 0.0), axis=1, keepdims=True))
    first_item = me * NI
    loads[5].wait()
    loads[6].wait()

    @pl.loop(0, NB, unroll=4)
    def _(b):
        at = pl.ds(pl.multiple_of(b * QB, QB), QB)
        q_rows = unit(queries[at, :].astype(F32))[0].astype(BF16)
        q_unit[at, :] = q_rows
        logits = dot_nt(cand_i[...], q_rows) * SCALE2 - shift_i
        hit = positive[:, at] == first_item + iota((NI, QB), 0)
        expo = jnp.exp2(logits)
        expo_i[:, at] = expo
        put_pair(sums_i, b, jnp.sum(expo, axis=0, keepdims=True))
        put_pair(pos.at[me], b, jnp.sum(jnp.where(hit, logits, 0.0), axis=0, keepdims=True))

    loads[7].wait()

    @pl.loop(0, ROWS // QB)
    def _(b):
        at = pl.ds(pl.multiple_of(b * QB, QB), QB)
        cache_unit[at, :] = unit(cache[at, :].astype(F32))[0].astype(BF16)

    @pl.loop(1, NC)
    def _(s):
        other = (me + s) % NC
        remote(msg.at[other], mrecv.at[other], m_s.at[other], m_r.at[other], col=other).wait()

    line = iota((8, 128), 0)
    asked = jnp.zeros((8, 128), F32)
    sum_i = jnp.zeros((8, 128), F32)
    sum_n = jnp.zeros((8, 128), F32)
    for g in range(8):
        four = (mrecv[4 * g] + mrecv[4 * g + 1]) + (mrecv[4 * g + 2] + mrecv[4 * g + 3])
        asked = jnp.where(line == g, four, asked)
        sum_i = sum_i + jnp.where(line == (g + 1) % 8, four, 0.0)
        sum_n = sum_n + jnp.where(line == (g + 2) % 8, four, 0.0)
    total_i = jnp.sum(sum_i, axis=0, keepdims=True)[:, 0:1]
    total_n = jnp.sum(sum_n, axis=0, keepdims=True)[:, 0:1]

    @pl.loop(1, NC)
    def _(s):
        to_all(pos, p_s, p_r, s).start()

    def parts(value):
        count = jnp.floor(value * (1.0 / ROWS))
        return count, (value - count * ROWS).astype(I32)

    by_slot = jnp.concatenate([asked, jnp.zeros((120, 128), F32)], axis=0).T
    for half in range(2):
        picks = []
        for g in range(4 * half, 4 * half + 4):
            count, wanted = parts(by_slot[:, g : g + 1])
            shift_n[g * 128 : (g + 1) * 128, :] = jnp.where(
                count > 0.5, jnp.log2(jnp.maximum(count, 1.0)), 1e30
            )
            picks.append(onehot(iota((128, ROWS), 1) == wanted))
        picked = dot_nn(jnp.concatenate(picks, axis=0), cache_unit[...])
        cand_n[half * 512 : (half + 1) * 512, :] = picked.astype(BF16)

    def tot_copy(half, s, mine):
        other = (me + s) % NC
        slot = me if mine else other
        return remote(
            tot.at[half, me], tot.at[half, slot], t_s.at[half, other], t_r.at[half, slot], col=other
        )

    def scores_n(half):
        @pl.loop(half * NB // 2, (half + 1) * NB // 2, unroll=4)
        def _(b):
            at = pl.ds(pl.multiple_of(b * QB, QB), QB)
            expo = jnp.exp2(dot_nt(cand_n[...], q_unit[at, :]) * SCALE2 - shift_n[...])
            expo_n[:, at] = expo
            sum_n = total_n * jnp.sum(expo, axis=0, keepdims=True)
            put_pair(tot.at[half, me], b - half * (NB // 2), total_i * pair_row(sums_i, b) + sum_n)

        @pl.loop(1, NC)
        def _(s):
            tot_copy(half, s, True).start()

    scores_n(0)
    scores_n(1)
    slots = parts(asked)[1]
    for g in range(8):
        scat[:, g * 128 : (g + 1) * 128] = onehot(iota((ROWS, 128), 0) == slots[g : g + 1, :])

    def sums_in(half):
        @pl.loop(1, NC)
        def _(s):
            tot_copy(half, s, False).wait()

        total = jnp.sum(tot[half], axis=0)
        factor_i[half * 8 : (half + 1) * 8] = total_i / total
        factor_n[half * 8 : (half + 1) * 8] = total_n / total
        loss_buf[half * 8 : (half + 1) * 8] = jnp.log(total)

    def factors(ref, half):
        return jnp.concatenate([ref[half * 8 + k : half * 8 + k + 1, :] for k in range(8)], axis=1)

    def grad_i(half):
        at = pl.ds(half * (NQ // 2), NQ // 2)
        factor = factors(factor_i, half)
        for b in range(2):
            rows = slice(b * (NI // 2), (b + 1) * (NI // 2))
            hit = positive[:, at] == first_item + b * (NI // 2) + iota((NI // 2, NQ // 2), 0)
            weights = (expo_i[rows, at] * factor - jnp.where(hit, 1.0, 0.0)).astype(BF16)
            weight_i[rows, at] = weights
            grad = dot_nn(weights, q_unit[at, :]) * INV_T
            for k in range(4):
                to = (k // 2, slice(b * (NZ // 2), (b + 1) * (NZ // 2)), slice((k % 2) * CH, (k % 2 + 1) * CH))
                piece = grad[:, k * W : (k + 1) * W].reshape(NZ // 2, CH, W)
                part_i[to] = piece if half == 0 else part_i[to] + piece

    def grad_n(half):
        at = pl.ds(half * (NQ // 2), NQ // 2)
        factor = factors(factor_n, half)
        for b in range(2):
            rows = slice(b * (NS // 2), (b + 1) * (NS // 2))
            weights = (expo_n[rows, at] * factor).astype(BF16)
            weight_n[rows, at] = weights
            grad = dot_nn(weights, q_unit[at, :]) * INV_T
            if half == 0:
                slot_grad[rows, :] = grad
            else:
                hi, lo = halves(slot_grad[rows, :] + grad)
                slot_hi[rows, :] = hi
                slot_lo[rows, :] = lo

    def ring_peer(d):
        return up if d == 0 else down

    def ring_chunk(d, t):
        return (z + 4 - t) % NZ if d == 0 else (z + 4 + t) % NZ

    def streams(n, d):
        mine = [(k, 4) for k in range(n) if 2 * k // n == d]
        return mine + [(k, 3) for k in range(n) if 2 * k // n != d]

    def both_ways(n):
        for one, two in zip(streams(n, 0), streams(n, 1)):
            yield (0,) + one
            yield (1,) + two

    def pack(ref, chunk):
        code, e = encode(chunk, 16)
        ref[0:CR] = code
        ref[CR:] = to_i16(e)

    def unpack(ref):
        return decode(ref[0:CR], from_i16(ref[CR:]))

    def pack_two(ref, chunk):
        code, e = encode(chunk[0:CH], 8)
        code2, e2 = encode(chunk[CH:], 8)
        ref[0:CH] = code
        ref[CH : 2 * CH] = code2
        ref[2 * CH :] = to_i16(jnp.concatenate([e, e2], axis=0))

    def unpack_two(ref):
        e = from_i16(ref[2 * CH :])
        return jnp.concatenate([decode(ref[0:CH], e[0:8]), decode(ref[CH : 2 * CH], e[8:])], axis=0)

    def ring_copy(kind, d, t, k):
        _, send, recv, s, r = kind[:5]
        return remote(send.at[d, t, k], recv.at[d, t, k], s.at[d, t, k], r.at[d, t, k], pb=ring_peer(d))

    def ring_first(kind, t):
        part, send, _, _, _, n, put, _ = kind
        for d, k, steps in both_ways(n):
            if steps + t == 4:
                put(send.at[d, t, k], part[k, ring_chunk(d, t)])
                ring_copy(kind, d, t, k).start()

    def ring_step(kind, t):
        part, send, recv, _, _, n, put, get = kind
        for d, k, steps in both_ways(n):
            if steps + t > 4:
                ring_copy(kind, d, t - 1, k).wait()
                put(send.at[d, t, k], part[k, ring_chunk(d, t)] + get(recv.at[d, t - 1, k]))
                ring_copy(kind, d, t, k).start()

    def ring_last(kind):
        part, _, recv, _, _, n, _, get = kind
        own = [part[k, z] for k in range(n)]
        for d, k, _ in both_ways(n):
            ring_copy(kind, d, 3, k).wait()
            own[k] = own[k] + get(recv.at[d, 3, k])
        return own

    kind_i = (part_i, send_i, recv_i, ri_s, ri_r, 2, pack_two, unpack_two)
    kind_n = (part_n, send_n, recv_n, rn_s, rn_r, 4, pack, unpack)

    def by_row(pair):
        at = pl.ds(pl.multiple_of(pair * 256, 256), 256)
        grad = dot_nn(scat[at, :], slot_hi[...]) + dot_nn(scat[at, :], slot_lo[...])
        for k in range(4):
            part_n[k, pl.ds(pair * 2, 2)] = grad[:, k * W : (k + 1) * W].reshape(2, CR, W)

    def q_which(i):
        return (chip // 2 + i) % NB

    def q_copy(i):
        two = pl.ds(q_which(i) * 2, 2)
        return remote(q_part.at[two, 1 - core], q_core.at[two], qc_s.at[i], qc_r.at[i], col=sibling)

    def q_block(i):
        b = q_which(i)
        at = pl.ds(pl.multiple_of(b * QB, QB), QB)
        grad = dot_tn(weight_i[:, at], cand_i[...]) + dot_tn(weight_n[:, at], cand_n[...])
        q_part[pl.ds(b * 2, 2)] = (grad * INV_T).reshape(2, 2, CH, E)
        q_copy(i).start()

    def q_send(i):
        q_copy(i).wait()
        for j in range(2):
            c = q_which(i) * 2 + j
            grad = q_part[c, core] + q_core[c]
            pack_two(q_msg.at[c], jnp.concatenate([grad[:, :H], grad[:, H:]], axis=0))

            @pl.when(c != chip)
            def _():
                remote(q_msg.at[c], q_recv.at[chip], qd_s.at[c], qd_r.at[chip], col=c * 2 + core).start()

            @pl.when(c == chip)
            def _():
                q_recv[chip] = q_msg[c]

    def out_copy(kind, p, k):
        ref, _, _, out, sem, _ = kind
        return pltpu.make_async_copy(ref.at[p, k], out.at[p, k], sem.at[p, k])

    def behind(d, s):
        return (z + 2 * NZ - s) % NZ if d == 0 else (z + s) % NZ

    def gather_copy(kind, d, s, k):
        ref, send, recv = kind[:3]
        ref = ref.at[behind(d, s), k]
        return remote(ref, ref, send.at[d, s, k], recv.at[d, s, k], pb=ring_peer(d))

    def gather_first(kind, k):
        for d in range(2):
            gather_copy(kind, d, 0, k).start()
        out_copy(kind, z, k).start()

    def gather_wait(kind, d, s, k):
        gather_copy(kind, d, s, k).wait()
        out_copy(kind, behind(d, s + 1), k).start()

    def gather_step(kind, s):
        for d, k, steps in both_ways(kind[5]):
            if s < steps:
                gather_wait(kind, d, s - 1, k)
                gather_copy(kind, d, s, k).start()

    def gather_last(kind):
        for three in (3, 4):
            for d, k, steps in both_ways(kind[5]):
                if steps == three:
                    gather_wait(kind, d, steps - 1, k)

    out_i = (ag_item, ai_s, ai_r, item_codes, oi_s, 2)
    out_n = (ag_cache, ac_s, ac_r, cache_codes, oc_s, 4)

    sums_in(0)
    grad_n(0)
    sums_in(1)
    grad_n(1)
    pair = ((z + 4) % NZ) // 2
    by_row(pair)
    ring_first(kind_n, 0)
    grad_i(0)
    grad_i(1)
    ring_first(kind_i, 0)
    ring_first(kind_i, 1)
    by_row((pair + 3) % 4)
    by_row((pair + 1) % 4)
    ring_first(kind_n, 1)
    ring_step(kind_n, 1)
    by_row((pair + 2) % 4)
    ring_step(kind_i, 1)
    q_block(0)
    q_block(1)
    q_block(2)
    ring_step(kind_n, 2)
    ring_step(kind_i, 2)
    q_block(3)
    q_block(4)
    q_send(0)
    ring_step(kind_n, 3)
    ring_step(kind_i, 3)
    q_block(5)
    q_block(6)
    q_block(7)
    q_send(1)

    own = jnp.concatenate(ring_last(kind_n), axis=1)
    grad = unit_back(own, cache[pl.ds(pl.multiple_of(z * CR, CR), CR), :].astype(F32))
    for k in range(4):
        pack(ag_cache.at[z, k], grad[:, k * W : (k + 1) * W])
        gather_first(out_n, k)

    own = ring_last(kind_i)
    own = jnp.concatenate([own[0][0:CH], own[0][CH:], own[1][0:CH], own[1][CH:]], axis=1)
    grad = unit_back(own, items[pl.ds(pl.multiple_of(z * CH, CH), CH), :].astype(F32))
    for h in range(2):
        left, right = grad[:, 2 * h * W : (2 * h + 1) * W], grad[:, (2 * h + 1) * W : (2 * h + 2) * W]
        pack_two(ag_item.at[z, h], jnp.concatenate([left, right], axis=0))
        gather_first(out_i, h)

    q_send(2)
    q_send(3)
    q_send(4)
    gather_step(out_n, 1)
    gather_step(out_i, 1)
    q_send(5)
    q_send(6)
    q_send(7)
    gather_step(out_n, 2)
    gather_step(out_i, 2)

    @pl.loop(1, NC)
    def _(s):
        from_all(pos, p_s, p_r, s).wait()

    loss_buf[...] = loss_buf[...] - (jnp.sum(pos[...], axis=0) * LN2 + jnp.log(total_i))
    loss_copy = pltpu.make_async_copy(loss_buf, loss_out, out_s.at[0])
    loss_copy.start()
    gather_step(out_n, 3)
    gather_step(out_i, 3)

    @pl.loop(1, NC // 2)
    def _(s):
        other = (chip + s) % (NC // 2)
        remote(q_msg.at[other], q_recv.at[other], qd_s.at[other], qd_r.at[other], col=other * 2 + core).wait()

    q_grad = unpack_two(q_recv.at[0])
    for c in range(1, NC // 2):
        q_grad = q_grad + unpack_two(q_recv.at[c])
    q_grad = jnp.concatenate([q_grad[0:CH], q_grad[CH:]], axis=1)
    query_buf[...] = unit_back(q_grad, queries[pl.ds(pl.multiple_of(me * CH, CH), CH), :].astype(F32))
    query_copy = pltpu.make_async_copy(query_buf, query_out, out_s.at[1])
    query_copy.start()

    gather_last(out_n)
    gather_last(out_i)

    @pl.loop(0, NZ)
    def _(p):
        for kind in (out_i, out_n):
            for k in range(kind[5]):
                out_copy(kind, p, k).wait()

    loss_copy.wait()
    query_copy.wait()


def last(loss, query, item_codes, cache_codes, loss_out, query_out, item_out, cache_out):
    for p in range(PB):
        for k in range(4):
            columns = slice(k * W, (k + 1) * W)
            part = k % 2
            e = from_i16(item_codes[p, k // 2, CR:])[8 * part : 8 * part + 8]
            item_out[p * CH : (p + 1) * CH, columns] = decode(item_codes[p, k // 2, part * CH : part * CH + CH], e)
            cache_out[p * CR : (p + 1) * CR, columns] = decode(
                cache_codes[p, k, 0:CR], from_i16(cache_codes[p, k, CR:])
            )

    @pl.when(pl.program_id(0) == 0)
    def _():
        loss_out[...] = loss[...]
        query_out[...] = query[...]


def body(queries, positive, items, item_counts, cache, neg_owner, neg_row, neg_counts):
    hbm = pl.BlockSpec(memory_space=pl.ANY)
    dma = pltpu.SemaphoreType.DMA
    codes_i = (NZ, 2, CR + 16, W)
    codes_n = (NZ, 4, CR + 16, W)
    ring_i = (2, 4, 2, CR + 16, W)
    ring_n = (2, 4, 4, CR + 16, W)
    scratch = [
        pltpu.VMEM((NQ, E), BF16),
        pltpu.VMEM((1, NQ), I32),
        pltpu.VMEM((NI, E), BF16),
        pltpu.VMEM((1, NI), I32),
        pltpu.VMEM((1, NN), I32),
        pltpu.VMEM((1, NN), I32),
        pltpu.VMEM((1, NN), I32),
        pltpu.VMEM((ROWS, E), BF16),
        pltpu.VMEM((NQ // 128, 128), F32),
        pltpu.VMEM((CH, E), F32),
        pltpu.VMEM((NC, 8, 128), F32),
        pltpu.VMEM((NC, 8, 128), F32),
        pltpu.VMEM((ROWS, E), BF16),
        pltpu.VMEM((ROWS, NS), BF16),
        pltpu.VMEM((NQ, E), BF16),
        pltpu.VMEM((NI, E), BF16),
        pltpu.VMEM((NS, E), BF16),
        pltpu.VMEM((NS, 1), F32),
        pltpu.VMEM((NI, NQ), F32),
        pltpu.VMEM((NS, NQ), F32),
        pltpu.VMEM((NC, NQ // 128, 128), F32),
        pltpu.VMEM((2, NC, NQ // 256, 128), F32),
        pltpu.VMEM((NQ // 128, 128), F32),
        pltpu.VMEM((NQ // 128, 128), F32),
        pltpu.VMEM((NQ // 128, 128), F32),
        pltpu.VMEM((NI, NQ), BF16),
        pltpu.VMEM((NS, NQ), BF16),
        pltpu.VMEM((2, NZ, 2 * CH, W), F32),
        pltpu.VMEM((4, NZ, CR, W), F32),
        pltpu.VMEM((NS, E), F32),
        pltpu.VMEM((NS, E), BF16),
        pltpu.VMEM((NS, E), BF16),
        pltpu.VMEM(ring_i, I16),
        pltpu.VMEM(ring_i, I16),
        pltpu.VMEM(ring_n, I16),
        pltpu.VMEM(ring_n, I16),
        pltpu.VMEM(codes_i, I16),
        pltpu.VMEM(codes_n, I16),
        pltpu.VMEM((NC // 2, 2, CH, E), F32),
        pltpu.VMEM((NC // 2, CH, E), F32),
        pltpu.VMEM((NC // 2, 2 * CH + 16, H), I16),
        pltpu.VMEM((NC // 2, 2 * CH + 16, H), I16),
        dma((8,)),
        dma((NC,)), dma((NC,)),
        dma((NC,)), dma((NC,)),
        dma((2, NC)), dma((2, NC)),
        dma((2, 4, 2)), dma((2, 4, 2)),
        dma((2, 4, 4)), dma((2, 4, 4)),
        dma((2, 4, 2)), dma((2, 4, 2)),
        dma((2, 4, 4)), dma((2, 4, 4)),
        dma((NZ, 2)), dma((NZ, 4)),
        dma((NB,)), dma((NB,)),
        dma((NC // 2,)), dma((NC // 2,)),
        dma((2,)),
    ]
    loss, query_grad, item_codes, cache_codes = pl.pallas_call(
        kernel,
        out_shape=(
            jax.ShapeDtypeStruct((NQ // 128, 128), F32),
            jax.ShapeDtypeStruct((CH, E), F32),
            jax.ShapeDtypeStruct(codes_i, I16),
            jax.ShapeDtypeStruct(codes_n, I16),
        ),
        in_specs=[hbm] * 8,
        out_specs=(hbm,) * 4,
        scratch_shapes=scratch,
        compiler_params=pltpu.CompilerParams(
            collective_id=0, has_side_effects=True, vmem_limit_bytes=62 * 1024 * 1024
        ),
    )(
        queries,
        positive.reshape(1, NQ),
        items,
        item_counts.reshape(1, NI),
        neg_counts.reshape(1, NN),
        neg_owner.reshape(1, NN),
        neg_row.reshape(1, NN),
        cache,
    )

    def whole(*shape):
        return pl.BlockSpec(shape, lambda r: (0,) * len(shape))

    def chunks(shape):
        return pl.BlockSpec((PB,) + shape[1:], lambda r: (r, 0, 0, 0))

    loss, query_grad, item_grad, cache_grad = pl.pallas_call(
        last,
        grid=(NZ // PB,),
        out_shape=(
            jax.ShapeDtypeStruct((NQ // 128, 128), F32),
            jax.ShapeDtypeStruct((CH, E), F32),
            jax.ShapeDtypeStruct((NI, E), F32),
            jax.ShapeDtypeStruct((ROWS, E), F32),
        ),
        in_specs=[whole(NQ // 128, 128), whole(CH, E), chunks(codes_i), chunks(codes_n)],
        out_specs=(
            whole(NQ // 128, 128),
            whole(CH, E),
            pl.BlockSpec((PB * CH, E), lambda r: (r, 0)),
            pl.BlockSpec((PB * CR, E), lambda r: (r, 0)),
        ),
        compiler_params=pltpu.CompilerParams(vmem_limit_bytes=62 * 1024 * 1024),
    )(loss, query_grad, item_codes, cache_codes)
    return loss.reshape(NQ), query_grad, item_grad, cache_grad


def solution(mesh):
    placed = (
        P("pb", None),
        P("pb"),
        P("col", None),
        P("col"),
        P("col", None),
        P("col", None),
        P("col"),
        P("col"),
    )
    return jax.shard_map(
        body,
        mesh=mesh,
        in_specs=placed,
        out_specs=(P("pb"), P(("pb", "col"), None), P("col", None), P("col", None)),
        check_vma=False,
    )
```

profile of v0, /device:TPU:32, one launch (start us, length us, event | category | flops | bytes accessed | tf_op | source)
XLA Modules:
  0.0 74.3 jit_solution(12262724023086530869)
XLA Ops:
  0.6 70.5 %shard_map.111 = (f32[16,128]{1,0:T(8,128)}, f32[64,512]{1,0:T(8,128)}, s16[8,2,144,128]{3,2,1,0:T(8,128)(2,1)}, s16[8,4,144,128]{3,2,1,0:T(8,128)(2,1)}) custom-call(bf16[2048,512]{1,0:T(8,128)(2,1)} %queries_hbm.1, s32[1,2048]{1,0:T(1,128)} %bitcast.6, bf16[512,512]{1,0:T(8,128)(2,1)} %items_hbm.1, s32[1,512]{1,0:T(1,128)} %bitcast.7, s32[1,512]{1,0:T(1,128)} %bitcast.8, ...), custom_call_target="tpu_custom_call" | custom-call | tf_op jit(solution)/shard_map/pallas_call | solution.py:630
  71.1 3.2 %shard_map.112 = (f32[16,128]{1,0:T(8,128)}, f32[64,512]{1,0:T(8,128)}, f32[512,512]{1,0:T(8,128)}, f32[1024,512]{1,0:T(8,128)}) custom-call(f32[16,128]{1,0:T(8,128)} %get-tuple-element.12.loss, f32[64,512]{1,0:T(8,128)} %get-tuple-element.13.query, s16[8,2,144,128]{3,2,1,0:T(8,128)(2,1)} %get-tuple-element.14.item_codes, ...), custom_call_target="tpu_custom_call" | custom-call | tf_op jit(solution)/shard_map/pallas_call | solution.py:661
where the time goes:
time: 74.4 us; the launch traced here: 74.3 us
  Pallas kernels  73.6 us (99%)
    pallas_call x1, Pallas kernels, body(): pl.pallas_call(kernel, out_shape=(jax.ShapeDtypeStruct((NQ // 128, 128),...  70.5 us
    pallas_call x1, Pallas kernels, body(): pl.pallas_call(last, grid=(NZ // PB,), out_shape=(jax.ShapeDtypeStruct((N...  3.16 us

commit v1 on v0

--- a/solution.py
+++ b/solution.py
@@ -63,6 +63,17 @@
     top = jnp.max(jnp.abs(cube), axis=0)
     expo = jnp.ceil(jnp.log2(jnp.maximum(top, 1e-30)))
     code = jnp.round(cube * jnp.exp2(14.99 - expo)[None])
+    return code.reshape(rows, width).astype(I32).astype(I16), expo
+
+
+def encode4(x):
+    rows, width = x.shape
+    cube = x.reshape(rows // 8, 8, width)
+    top = jnp.max(jnp.abs(cube), axis=0)
+    top = jnp.maximum(top[0:4], top[4:8])
+    expo = jnp.ceil(jnp.log2(jnp.maximum(top, 1e-30)))
+    scale = jnp.exp2(14.99 - jnp.concatenate([expo, expo], axis=0))
+    code = jnp.round(cube * scale[None])
     return code.reshape(rows, width).astype(I32).astype(I16), expo
 
 
@@ -231,10 +242,6 @@
     total_i = jnp.sum(sum_i, axis=0, keepdims=True)[:, 0:1]
     total_n = jnp.sum(sum_n, axis=0, keepdims=True)[:, 0:1]
 
-    @pl.loop(1, NC)
-    def _(s):
-        to_all(pos, p_s, p_r, s).start()
-
     def parts(value):
         count = jnp.floor(value * (1.0 / ROWS))
         return count, (value - count * ROWS).astype(I32)
@@ -273,6 +280,11 @@
 
     scores_n(0)
     scores_n(1)
+
+    @pl.loop(1, NC)
+    def _(s):
+        to_all(pos, p_s, p_r, s).start()
+
     slots = parts(asked)[1]
     for g in range(8):
         scat[:, g * 128 : (g + 1) * 128] = onehot(iota((ROWS, 128), 0) == slots[g : g + 1, :])
@@ -383,11 +395,11 @@
     kind_i = (part_i, send_i, recv_i, ri_s, ri_r, 2, pack_two, unpack_two)
     kind_n = (part_n, send_n, recv_n, rn_s, rn_r, 4, pack, unpack)
 
-    def by_row(pair):
-        at = pl.ds(pl.multiple_of(pair * 256, 256), 256)
+    def by_row(first, count):
+        at = pl.ds(pl.multiple_of(first * CR, CR), count * CR)
         grad = dot_nn(scat[at, :], slot_hi[...]) + dot_nn(scat[at, :], slot_lo[...])
         for k in range(4):
-            part_n[k, pl.ds(pair * 2, 2)] = grad[:, k * W : (k + 1) * W].reshape(2, CR, W)
+            part_n[k, pl.ds(first, count)] = grad[:, k * W : (k + 1) * W].reshape(count, CR, W)
 
     def q_which(i):
         return (chip // 2 + i) % NB
@@ -459,17 +471,18 @@
     sums_in(1)
     grad_n(1)
     pair = ((z + 4) % NZ) // 2
-    by_row(pair)
+    by_row((z + 4) % NZ, 1)
     ring_first(kind_n, 0)
     grad_i(0)
     grad_i(1)
     ring_first(kind_i, 0)
     ring_first(kind_i, 1)
-    by_row((pair + 3) % 4)
-    by_row((pair + 1) % 4)
+    by_row(2 * pair + 1 - z % 2, 1)
+    by_row(2 * ((pair + 3) % 4), 2)
+    by_row(2 * ((pair + 1) % 4), 2)
     ring_first(kind_n, 1)
     ring_step(kind_n, 1)
-    by_row((pair + 2) % 4)
+    by_row(2 * ((pair + 2) % 4), 2)
     ring_step(kind_i, 1)
     q_block(0)
     q_block(1)
@@ -486,18 +499,25 @@
     q_block(7)
     q_send(1)
 
+    cache_e = []
     own = jnp.concatenate(ring_last(kind_n), axis=1)
     grad = unit_back(own, cache[pl.ds(pl.multiple_of(z * CR, CR), CR), :].astype(F32))
     for k in range(4):
-        pack(ag_cache.at[z, k], grad[:, k * W : (k + 1) * W])
+        code, e = encode4(grad[:, k * W : (k + 1) * W])
+        ag_cache[z, k] = code
         gather_first(out_n, k)
+        cache_e.append(e)
 
     own = ring_last(kind_i)
     own = jnp.concatenate([own[0][0:CH], own[0][CH:], own[1][0:CH], own[1][CH:]], axis=1)
     grad = unit_back(own, items[pl.ds(pl.multiple_of(z * CH, CH), CH), :].astype(F32))
     for h in range(2):
-        left, right = grad[:, 2 * h * W : (2 * h + 1) * W], grad[:, (2 * h + 1) * W : (2 * h + 2) * W]
-        pack_two(ag_item.at[z, h], jnp.concatenate([left, right], axis=0))
+        e = []
+        for k in range(2):
+            code, e_item = encode4(grad[:, (2 * h + k) * W : (2 * h + k + 1) * W])
+            ag_item[z, h, k * CH : (k + 1) * CH] = code
+            e.append(e_item)
+        ag_item[z, h, CR:] = to_i16(jnp.concatenate(e + cache_e[2 * h : 2 * h + 2], axis=0))
         gather_first(out_i, h)
 
     q_send(2)
@@ -552,11 +572,13 @@
         for k in range(4):
             columns = slice(k * W, (k + 1) * W)
             part = k % 2
-            e = from_i16(item_codes[p, k // 2, CR:])[8 * part : 8 * part + 8]
-            item_out[p * CH : (p + 1) * CH, columns] = decode(item_codes[p, k // 2, part * CH : part * CH + CH], e)
-            cache_out[p * CR : (p + 1) * CR, columns] = decode(
-                cache_codes[p, k, 0:CR], from_i16(cache_codes[p, k, CR:])
-            )
+            e = from_i16(item_codes[p, k // 2, CR:])
+            e_item = e[4 * part : 4 * part + 4]
+            e_cache = e[8 + 4 * part : 12 + 4 * part]
+            code = item_codes[p, k // 2, part * CH : part * CH + CH]
+            item_out[p * CH : (p + 1) * CH, columns] = decode(code, jnp.concatenate([e_item, e_item], axis=0))
+            code = cache_codes[p, k]
+            cache_out[p * CR : (p + 1) * CR, columns] = decode(code, jnp.concatenate([e_cache, e_cache], axis=0))
 
     @pl.when(pl.program_id(0) == 0)
     def _():
@@ -568,7 +590,7 @@
     hbm = pl.BlockSpec(memory_space=pl.ANY)
     dma = pltpu.SemaphoreType.DMA
     codes_i = (NZ, 2, CR + 16, W)
-    codes_n = (NZ, 4, CR + 16, W)
+    codes_n = (NZ, 4, CR, W)
     ring_i = (2, 4, 2, CR + 16, W)
     ring_n = (2, 4, 4, CR + 16, W)
     scratch = [

time: 74.4 us -> 72.3 us (0.972)
  Pallas kernels: 73.6 us -> 71.5 us
    pallas_call x1, Pallas kernels: 70.5 us -> 68.4 us  [body(): pl.pallas_call(kernel, out_shape=(jax.ShapeDtypeStruct((NQ // 128, 128),...]
where the time goes in v1:
time: 72.3 us; the launch traced here: 72.2 us
  Pallas kernels  71.5 us (99%)
    pallas_call x1, Pallas kernels, body(): pl.pallas_call(kernel, out_shape=(jax.ShapeDtypeStruct((NQ // 128, 128),...  68.4 us
    pallas_call x1, Pallas kernels, body(): pl.pallas_call(last, grid=(NZ // PB,), out_shape=(jax.ShapeDtypeStruct((N...  3.16 us

profile of v1, /device:TPU:32, one launch (start us, length us, event | category | flops | bytes accessed | tf_op | source)
XLA Modules:
  0.0 72.2 jit_solution(7925667382224845239)
XLA Ops:
  0.6 68.4 %shard_map.111 = (f32[16,128]{1,0:T(8,128)}, f32[64,512]{1,0:T(8,128)}, s16[8,2,144,128]{3,2,1,0:T(8,128)(2,1)}, s16[8,4,128,128]{3,2,1,0:T(8,128)(2,1)}) custom-call(bf16[2048,512]{1,0:T(8,128)(2,1)} %queries_hbm.1, s32[1,2048]{1,0:T(1,128)} %bitcast.6, bf16[512,512]{1,0:T(8,128)(2,1)} %items_hbm.1, s32[1,512]{1,0:T(1,128)} %bitcast.7, s32[1,512]{1,0:T(1,128)} %bitcast.8, ...), custom_call_target="tpu_custom_call" | custom-call | tf_op jit(solution)/shard_map/pallas_call | solution.py:652
  69.0 3.2 %shard_map.112 = (f32[16,128]{1,0:T(8,128)}, f32[64,512]{1,0:T(8,128)}, f32[512,512]{1,0:T(8,128)}, f32[1024,512]{1,0:T(8,128)}) custom-call(f32[16,128]{1,0:T(8,128)} %get-tuple-element.12.loss, f32[64,512]{1,0:T(8,128)} %get-tuple-element.13.query, s16[8,2,144,128]{3,2,1,0:T(8,128)(2,1)} %get-tuple-element.14.item_codes, ...), custom_call_target="tpu_custom_call" | custom-call | tf_op jit(solution)/shard_map/pallas_call | solution.py:683

commit v2 on v1

--- a/solution.py
+++ b/solution.py
@@ -395,11 +395,12 @@
     kind_i = (part_i, send_i, recv_i, ri_s, ri_r, 2, pack_two, unpack_two)
     kind_n = (part_n, send_n, recv_n, rn_s, rn_r, 4, pack, unpack)
 
-    def by_row(first, count):
-        at = pl.ds(pl.multiple_of(first * CR, CR), count * CR)
+    def by_row(away):
+        chunk = (z + away) % NZ
+        at = pl.ds(pl.multiple_of(chunk * CR, CR), CR)
         grad = dot_nn(scat[at, :], slot_hi[...]) + dot_nn(scat[at, :], slot_lo[...])
         for k in range(4):
-            part_n[k, pl.ds(first, count)] = grad[:, k * W : (k + 1) * W].reshape(count, CR, W)
+            part_n[k, chunk] = grad[:, k * W : (k + 1) * W]
 
     def q_which(i):
         return (chip // 2 + i) % NB
@@ -470,20 +471,22 @@
     grad_n(0)
     sums_in(1)
     grad_n(1)
-    pair = ((z + 4) % NZ) // 2
-    by_row((z + 4) % NZ, 1)
+    by_row(4)
     ring_first(kind_n, 0)
+    by_row(3)
+    by_row(5)
+    ring_first(kind_n, 1)
     grad_i(0)
     grad_i(1)
     ring_first(kind_i, 0)
     ring_first(kind_i, 1)
-    by_row(2 * pair + 1 - z % 2, 1)
-    by_row(2 * ((pair + 3) % 4), 2)
-    by_row(2 * ((pair + 1) % 4), 2)
-    ring_first(kind_n, 1)
     ring_step(kind_n, 1)
-    by_row(2 * ((pair + 2) % 4), 2)
+    by_row(2)
+    by_row(6)
     ring_step(kind_i, 1)
+    by_row(1)
+    by_row(7)
+    by_row(0)
     q_block(0)
     q_block(1)
     q_block(2)

time: 72.3 us -> 73.2 us (1.012)
  no operation moved by 1% of the time
where the time goes in v2:
time: 73.2 us; the launch traced here: 72.8 us
  Pallas kernels  72.2 us (99%)
    pallas_call x1, Pallas kernels, body(): pl.pallas_call(kernel, out_shape=(jax.ShapeDtypeStruct((NQ // 128, 128),...  69 us
    pallas_call x1, Pallas kernels, body(): pl.pallas_call(last, grid=(NZ // PB,), out_shape=(jax.ShapeDtypeStruct((N...  3.16 us

profile of v2, /device:TPU:32, one launch (start us, length us, event | category | flops | bytes accessed | tf_op | source)
XLA Modules:
  0.0 72.8 jit_solution(13627770744077565178)
XLA Ops:
  0.6 69.0 %shard_map.111 = (f32[16,128]{1,0:T(8,128)}, f32[64,512]{1,0:T(8,128)}, s16[8,2,144,128]{3,2,1,0:T(8,128)(2,1)}, s16[8,4,128,128]{3,2,1,0:T(8,128)(2,1)}) custom-call(bf16[2048,512]{1,0:T(8,128)(2,1)} %queries_hbm.1, s32[1,2048]{1,0:T(1,128)} %bitcast.6, bf16[512,512]{1,0:T(8,128)(2,1)} %items_hbm.1, s32[1,512]{1,0:T(1,128)} %bitcast.7, s32[1,512]{1,0:T(1,128)} %bitcast.8, ...), custom_call_target="tpu_custom_call" | custom-call | tf_op jit(solution)/shard_map/pallas_call | solution.py:655
  69.7 3.2 %shard_map.112 = (f32[16,128]{1,0:T(8,128)}, f32[64,512]{1,0:T(8,128)}, f32[512,512]{1,0:T(8,128)}, f32[1024,512]{1,0:T(8,128)}) custom-call(f32[16,128]{1,0:T(8,128)} %get-tuple-element.12.loss, f32[64,512]{1,0:T(8,128)} %get-tuple-element.13.query, s16[8,2,144,128]{3,2,1,0:T(8,128)(2,1)} %get-tuple-element.14.item_codes, ...), custom_call_target="tpu_custom_call" | custom-call | tf_op jit(solution)/shard_map/pallas_call | solution.py:686
